TPU v7x, 256 devices: a whole 4x4x8 slice. The times are simulated.
256 devices in a mesh: samp: 2 (over x_lo), lat: 16 (over z, core), lon: 8 (over x_hi, y).
Axes of the slice: x: 4 (x_hi: 2, x_lo: 2; x = x_hi * 2 + x_lo), y: 4, z: 8, core: 2. Of those that a mesh axis runs over, the one named last changes fastest.
Arguments:
- tokens: bfloat16 [512, 512, 512], P(('samp', 'lat'), 'lon'), parts along dimension 0, may hold values from -6 to 6
- block_gain: float32 [512], replicated, may hold values from 0.25 to 1.75
- block_qkv: bfloat16 [512, 1536], replicated, may hold values from -16 to 16
- block_out: bfloat16 [512, 512], replicated, may hold values from -0.25 to 0.25
- grid_gain: float32 [512], replicated, may hold values from 0.25 to 1.75
- grid_qkv: bfloat16 [512, 1536], replicated, may hold values from -16 to 16
- grid_out: bfloat16 [512, 512], replicated, may hold values from -0.25 to 0.25
- mlp_gain: float32 [512], replicated, may hold values from 0.25 to 1.75
- w_up: bfloat16 [512, 2048], replicated, may hold values from -0.25 to 0.25
- w_down: bfloat16 [2048, 512], replicated, may hold values from -0.125 to 0.125
Outputs:
- blocks_out: bfloat16 [512, 512, 512], P(('samp', 'lat'), 'lon'), parts along dimension 0
There are 2 independent parts, one for each index of `samp`. A program takes and returns all parts, laid end to end along the dimension named above; an argument that names none is the same for every part. Nothing has to cross between parts.
All inputs are finite; a program needn't handle non-finite values.
Results may differ from a plain program's by a relative error of at most 0.015.
Values may be sent and summed in bfloat16 or wider, within the bound.
A program may use at most 64 MiB of HBM per device.

v0:
```python
import math

import jax
import jax.numpy as jnp
from jax import lax
from jax.sharding import PartitionSpec as P

HEADS = 16
WIN = 8


def layer_norm(tile, gain):
    values = tile.astype(jnp.float32)
    row_mean = jnp.mean(values, axis=-1, keepdims=True)
    centred = values - row_mean
    spread = jnp.mean(centred * centred, axis=-1, keepdims=True)
    return (centred * lax.rsqrt(spread + 1e-05) * gain).astype(jnp.bfloat16)


def window_attention(windows, gain, w_qkv, w_proj):
    count, span, width = windows.shape
    head_size = width // HEADS
    normed = layer_norm(windows, gain)
    projected = jnp.dot(
        normed.reshape(count * span, width), w_qkv, preferred_element_type=jnp.float32
    )
    projected = projected.astype(jnp.bfloat16).reshape(count, span, 3, HEADS, head_size)
    queries = projected[:, :, 0]
    keys_all = projected[:, :, 1]
    values_all = projected[:, :, 2]
    scores = jnp.einsum(
        "nqhe,nkhe->nhqk", queries, keys_all, preferred_element_type=jnp.float32
    ) * (1.0 / math.sqrt(head_size))
    weights_soft = jax.nn.softmax(scores, axis=-1).astype(jnp.bfloat16)
    mixed = jnp.einsum(
        "nhqk,nkhe->nqhe", weights_soft, values_all, preferred_element_type=jnp.float32
    )
    mixed = mixed.astype(jnp.bfloat16).reshape(count * span, width)
    result = jnp.dot(mixed, w_proj, preferred_element_type=jnp.float32).reshape(count, span, width)
    return (windows.astype(jnp.float32) + result).astype(jnp.bfloat16)


def to_blocks(tile):
    rows, cols, width = tile.shape
    shaped = tile.reshape(rows // WIN, WIN, cols // WIN, WIN, width)
    return shaped.transpose(0, 2, 1, 3, 4).reshape(-1, WIN * WIN, width)


def from_blocks(windows, rows, cols):
    width = windows.shape[-1]
    shaped = windows.reshape(rows // WIN, cols // WIN, WIN, WIN, width)
    return shaped.transpose(0, 2, 1, 3, 4).reshape(rows, cols, width)


def to_grid(tile):
    rows, cols, width = tile.shape
    shaped = tile.reshape(WIN, rows // WIN, WIN, cols // WIN, width)
    return shaped.transpose(1, 3, 0, 2, 4).reshape(-1, WIN * WIN, width)


def from_grid(windows, rows, cols):
    width = windows.shape[-1]
    shaped = windows.reshape(rows // WIN, cols // WIN, WIN, WIN, width)
    return shaped.transpose(2, 0, 3, 1, 4).reshape(rows, cols, width)


def send_out(tile):
    rows, cols, width = tile.shape
    lat_count = lax.axis_size("lat")
    lon_count = lax.axis_size("lon")
    row_share = rows // lat_count
    col_share = cols // lon_count
    pieces = tile.reshape(row_share, lat_count, col_share, lon_count, width).transpose(
        1, 3, 0, 2, 4
    )
    pieces = pieces.reshape(lat_count * lon_count, 1, row_share, col_share, width)
    moved = lax.all_to_all(pieces, ("lat", "lon"), split_axis=0, concat_axis=1, tiled=True)
    moved = moved.reshape(lat_count, lon_count, row_share, col_share, width).transpose(
        0, 2, 1, 3, 4
    )
    return moved.reshape(rows, cols, width)


def send_home(tile):
    rows, cols, width = tile.shape
    lat_count = lax.axis_size("lat")
    lon_count = lax.axis_size("lon")
    row_share = rows // lat_count
    col_share = cols // lon_count
    pieces = tile.reshape(lat_count, row_share, lon_count, col_share, width).transpose(
        0, 2, 1, 3, 4
    )
    pieces = pieces.reshape(lat_count * lon_count, 1, row_share, col_share, width)
    moved = lax.all_to_all(pieces, ("lat", "lon"), split_axis=0, concat_axis=1, tiled=True)
    moved = moved.reshape(lat_count, lon_count, row_share, col_share, width).transpose(
        2, 0, 3, 1, 4
    )
    return moved.reshape(rows, cols, width)


def feed_forward(tile, gain, w_up, w_down):
    rows, cols, width = tile.shape
    normed = layer_norm(tile, gain).reshape(rows * cols, width)
    hidden = jax.nn.gelu(
        jnp.dot(normed, w_up, preferred_element_type=jnp.float32), approximate=True
    ).astype(jnp.bfloat16)
    result = jnp.dot(hidden, w_down, preferred_element_type=jnp.float32).reshape(rows, cols, width)
    return (tile.astype(jnp.float32) + result).astype(jnp.bfloat16)


def shards(
    tokens, block_gain, block_qkv, block_out, grid_gain, grid_qkv, grid_out, mlp_gain, w_up, w_down
):
    rows, cols, width = tokens.shape
    after_block = from_blocks(
        window_attention(to_blocks(tokens), block_gain, block_qkv, block_out), rows, cols
    )
    gridded = send_out(after_block)
    attended = from_grid(
        window_attention(to_grid(gridded), grid_gain, grid_qkv, grid_out), rows, cols
    )
    after_grid = send_home(attended)
    return feed_forward(after_grid, mlp_gain, w_up, w_down)


def solution(mesh):
    in_specs = (P(("samp", "lat"), "lon", None), P(), P(), P(), P(), P(), P(), P(), P(), P())
    out_specs = P(("samp", "lat"), "lon", None)
    return jax.shard_map(shards, mesh=mesh, in_specs=in_specs, out_specs=out_specs, check_vma=False)
```

profile of v0, /device:TPU:32, one launch (start us, length us, event | category | flops | bytes accessed | tf_op | source)
XLA Modules:
  0.0 196.0 jit_solution(4437075312491168614)
XLA Ops:
  0.0 1.6 bitcast_reduce_fusion
  1.6 0.1 div.41
  1.7 0.0 copy-start.7
  1.7 1.7 fusion.35
  3.4 0.0 copy-done.4
  3.5 1.6 copy.123
  5.1 0.1 rsqrt.34
  5.2 0.0 copy-start.10
  5.2 2.1 %fusion.26 = bf16[1024,512]{1,0:T(8,128)(2,1)S(1)} fusion(f32[2,8,8,8,512]{4,3,1,2,0:T(8,128)} %copy.123, f32[512]{0:T(512)S(1)} %copy-done.7, f32[1024]{0:T(1024)S(1)} %rsqrt.34, f32[1024]{0:T(1024)S(1)} %div.41), kind=kLoop, calls=%fused_computation.37 | loop fusion | flops 2097152 | bytes 3155968 | tf_op jit(solution)/shard_map/convert_element_type | solution.py:17
  7.3 3.5 %convolution_convert_fusion.1 = bf16[1024,1536]{1,0:T(8,128)(2,1)} fusion(bf16[1024,512]{1,0:T(8,128)(2,1)S(1)} %fusion.26, bf16[512,1536]{1,0:T(8,128)(2,1)S(1)} %copy-done.10), kind=kOutput, calls=%fused_computation.25 | convolution fusion | flops 1612185600 | bytes 5767168 | tf_op jit(solution)/shard_map/dot_general | solution.py:24
  10.7 4.7 %copy.124 = bf16[1024,1536]{0,1:T(8,128)(2,1)} copy(bf16[1024,1536]{1,0:T(8,128)(2,1)} %convolution_convert_fusion.1) | data formatting | bytes 6291456 | tf_op jit(solution)/shard_map/convert_element_type | solution.py:27
  15.5 9.2 %reshape.181 = bf16[16,64,3,16,32]{1,0,4,3,2:T(8,128)(2,1)} reshape(bf16[1024,1536]{0,1:T(8,128)(2,1)} %copy.124) | data formatting | bytes 6291456 | tf_op jit(solution)/shard_map/reshape | solution.py:27
  24.7 4.5 %fusion.51 = (bf16[16,64,1,16,32]{1,0,4,3,2:T(8,128)(2,1)S(1)}, bf16[16,64,1,16,32]{1,0,4,3,2:T(8,128)(2,1)S(1)}, bf16[16,64,1,16,32]{1,0,4,3,2:T(8,128)(2,1)S(1)}) fusion(bf16[16,64,3,16,32]{1,0,4,3,2:T(8,128)(2,1)} %reshape.181), kind=kLoop, calls=%fused_computation.78 | loop fusion | bytes 6291456 | tf_op jit(solution)/shard_map/slice | solution.py:30
  29.1 1.9 fusion.23
  31.1 12.2 %fusion.52 = (f32[16,16,64]{2,1,0:T(8,128)S(1)}, f32[16,16,64,64]{2,3,1,0:T(8,128)S(1)}) fusion(f32[16,16,64,64]{2,3,1,0:T(8,128)S(1)} %fusion.23), kind=kOutput, calls=%fused_computation.79 | output fusion | flops 4194367 | bytes 8454144 | tf_op jit(solution)/shard_map/sub | solution.py:34
  43.2 0.0 copy-start.5
  43.2 1.5 fusion.39
  44.8 0.0 copy-done.1
  44.8 0.1 copy-done.5
  44.9 0.7 add_convert_fusion.1
  45.6 0.1 copy.130
  45.7 0.4 copy.131
  46.1 46.2 %all_to_all.8 = bf16[128,1,1,8,512]{4,3,2,1,0:T(8,128)(2,1)S(1)} all-to-all(bf16[128,1,1,8,512]{4,3,2,1,0:T(8,128)(2,1)S(1)} %bitcast.144), channel_id=1, replica_groups=mesh['samp'=2,'lat'=16,'lon'=8] {'lat','lon'}, dimensions={0} | all-to-all | bytes 2097152 | tf_op jit(solution)/shard_map/all_to_all | solution.py:77
  92.3 0.2 fusion.40
  92.6 0.1 copy.136
  92.7 0.1 div.46
  92.8 0.1 copy.137
  92.8 1.6 convert_bitcast_fusion.1
  94.5 0.5 multiply_reduce_fusion.3
  95.0 0.1 copy.138
  95.1 0.1 rsqrt.36
  95.2 0.0 copy-start.8
  95.2 2.8 %copy.134 = f32[2,8,8,8,512]{4,3,2,1,0:T(8,128)S(1)} copy(f32[2,8,8,8,512]{4,1,3,0,2:T(8,128)} %convert_bitcast_fusion.1) | data formatting | bytes 4194304 | tf_op jit(solution)/shard_map/convert_element_type | solution.py:40
  98.0 1.3 copy-done.2
  99.3 0.4 fusion.33
  99.7 1.0 copy-done.11
  100.7 3.5 %convolution_convert_fusion = bf16[1024,1536]{1,0:T(8,128)(2,1)} fusion(bf16[1024,512]{1,0:T(8,128)(2,1)S(1)} %fusion.33, bf16[512,1536]{1,0:T(8,128)(2,1)S(1)} %copy-done.11), kind=kOutput, calls=%fused_computation.24 | convolution fusion | flops 1612185600 | bytes 5767168 | tf_op jit(solution)/shard_map/dot_general | solution.py:24
  104.2 4.7 %copy.139 = bf16[1024,1536]{0,1:T(8,128)(2,1)} copy(bf16[1024,1536]{1,0:T(8,128)(2,1)} %convolution_convert_fusion) | data formatting | bytes 6291456 | tf_op jit(solution)/shard_map/convert_element_type | solution.py:27
  108.9 9.2 %reshape.184 = bf16[16,64,3,16,32]{1,0,4,3,2:T(8,128)(2,1)} reshape(bf16[1024,1536]{0,1:T(8,128)(2,1)} %copy.139) | data formatting | bytes 6291456 | tf_op jit(solution)/shard_map/reshape | solution.py:27
  118.1 4.5 %fusion.50 = (bf16[16,64,1,16,32]{1,0,4,3,2:T(8,128)(2,1)S(1)}, bf16[16,64,1,16,32]{1,0,4,3,2:T(8,128)(2,1)S(1)}, bf16[16,64,1,16,32]{1,0,4,3,2:T(8,128)(2,1)S(1)}) fusion(bf16[16,64,3,16,32]{1,0,4,3,2:T(8,128)(2,1)} %reshape.184), kind=kLoop, calls=%fused_computation.77 | loop fusion | bytes 6291456 | tf_op jit(solution)/shard_map/slice | solution.py:30
  122.6 1.9 fusion.22
  124.5 12.2 %fusion.53 = (f32[16,16,64]{2,1,0:T(8,128)S(1)}, f32[16,16,64,64]{2,3,1,0:T(8,128)S(1)}) fusion(f32[16,16,64,64]{2,3,1,0:T(8,128)S(1)} %fusion.22), kind=kOutput, calls=%fused_computation.80 | output fusion | flops 4194367 | bytes 8454144 | tf_op jit(solution)/shard_map/sub | solution.py:34
  136.7 0.0 copy-start.6
  136.7 1.5 fusion.38
  138.2 0.0 copy-done.3
  138.3 0.1 copy-done.6
  138.4 0.7 add_convert_fusion
  139.1 0.6 copy.145
  139.7 37.5 %all_to_all.9 = bf16[128,1,1,8,512]{4,3,2,1,0:T(8,128)(2,1)S(1)} all-to-all(bf16[128,1,1,8,512]{4,3,2,1,0:T(8,128)(2,1)S(1)} %bitcast.145), channel_id=1, replica_groups=mesh['samp'=2,'lat'=16,'lon'=8] {'lat','lon'}, dimensions={0} | all-to-all | bytes 2097152 | tf_op jit(solution)/shard_map/all_to_all | solution.py:94
  177.2 0.2 fusion.41
  177.4 0.1 copy.150
  177.5 0.1 copy.152
  177.6 0.1 copy.151
  177.7 1.6 convert_bitcast_fusion
  179.3 0.5 multiply_reduce_fusion.2
  179.8 0.1 copy.153
  180.0 0.1 copy.154
  180.1 0.1 rsqrt.38
  180.2 0.1 div.51
  180.2 0.0 copy-start.9
  180.3 3.2 %copy.148 = f32[1,16,8,8,512]{4,3,2,1,0:T(8,128)S(1)} copy(f32[1,16,8,8,512]{4,2,3,1,0:T(8,128)} %convert_bitcast_fusion) | data formatting | bytes 4194304 | tf_op jit(solution)/shard_map/convert_element_type | solution.py:108
  183.5 0.4 fusion.29
  183.9 7.7 %fusion.20 = f32[1024,512]{1,0:T(8,128)} fusion(bf16[2048,512]{1,0:T(8,128)(2,1)S(1)} %copy-done, bf16[1024,512]{1,0:T(8,128)(2,1)S(1)} %fusion.29, bf16[512,2048]{1,0:T(8,128)(2,1)} %param.18), kind=kOutput, calls=%fused_computation.23 | convolution fusion | flops 4313841664 | bytes 7340032 | tf_op jit(solution)/shard_map/dot_general | solution.py:107
  191.5 4.4 %fusion.30 = bf16[16,64,512]{2,1,0:T(8,128)(2,1)} fusion(f32[16,64,512]{2,1,0:T(8,128)} %bitcast.148, f32[1,16,8,8,512]{4,2,3,1,0:T(8,128)} %convert_bitcast_fusion), kind=kLoop, calls=%fused_computation.44 | loop fusion | flops 1048576 | bytes 5242880 | tf_op jit(solution)/shard_map/convert_element_type | solution.py:108
  (17 shorter events, 0.1 us)
Async XLA Ops:
  0.0 183.9 %copy-start = (bf16[2048,512]{1,0:T(8,128)(2,1)S(1)}, bf16[2048,512]{1,0:T(8,128)(2,1)}, u32[]{:S(2)}) copy-start(bf16[2048,512]{1,0:T(8,128)(2,1)} %param.19) | copy-start | bytes 6291460
  0.0 3.4 %copy-start.4 = (bf16[16,64,512]{2,1,0:T(8,128)(2,1)S(1)}, bf16[16,64,512]{2,1,0:T(8,128)(2,1)}, u32[]{:S(2)}) copy-start(bf16[16,64,512]{2,1,0:T(8,128)(2,1)} %param.10) | copy-start | bytes 3145732
  1.7 3.5 %copy-start.7 = (f32[512]{0:T(512)S(1)}, f32[512]{0:T(512)}, u32[]{:S(2)}) copy-start(f32[512]{0:T(512)} %param.11) | copy-start | bytes 6148
  5.2 2.1 %copy-start.10 = (bf16[512,1536]{1,0:T(8,128)(2,1)S(1)}, bf16[512,1536]{1,0:T(8,128)(2,1)}, u32[]{:S(2)}) copy-start(bf16[512,1536]{1,0:T(8,128)(2,1)} %param.12) | copy-start | bytes 4718596
  43.2 1.6 copy-start.1
  43.2 1.7 copy-start.5
  95.2 4.1 %copy-start.8 = (f32[512]{0:T(512)S(1)}, f32[512]{0:T(512)}, u32[]{:S(2)}) copy-start(f32[512]{0:T(512)} %param.14) | copy-start | bytes 6148
  98.0 1.3 copy-start.2
  99.3 1.4 copy-start.11
  136.7 1.6 copy-start.3
  136.7 1.7 copy-start.6
  180.2 3.2 %copy-start.9 = (f32[512]{0:T(512)S(1)}, f32[512]{0:T(512)}, u32[]{:S(2)}) copy-start(f32[512]{0:T(512)} %param.17) | copy-start | bytes 6148
where the time goes:
time: 198 us; the launch traced here: 196 us
  blocking collectives  83.7 us (42%)
  local copies, waits for them, and re-layouts  49.4 us (25%)
  other arithmetic  39.6 us (20%)
  matrix products  23 us (12%)
    all_to_all x1, blocking collectives, send_out(): lax.all_to_all(pieces, ('lat', 'lon'), split_axis=0, concat_axis=1, tiled...  46.2 us
    all_to_all x1, blocking collectives, send_home(): lax.all_to_all(pieces, ('lat', 'lon'), split_axis=0, concat_axis=1, tiled...  37.5 us
    sub x2, other arithmetic, window_attention(): weights_soft = jax.nn.softmax(scores, axis=-1).astype(jnp.bfloat16)  24.3 us
    reshape x2, local copies, waits for them, and re-layouts, window_attention(): projected.astype(jnp.bfloat16).reshape(count, span, 3, HEADS, head_size)  18.4 us
    convert_element_type x2, local copies, waits for them, and re-layouts, window_attention(): projected.astype(jnp.bfloat16).reshape(count, span, 3, HEADS, head_size)  9.46 us
    slice x2, local copies, waits for them, and re-layouts, window_attention(): values_all = projected[:, :, 2]  8.91 us
    dot_general x1, matrix products, feed_forward(): jnp.dot(hidden, w_down, preferred_element_type=jnp.float32)  7.66 us
    dot_general x2, matrix products, window_attention(): jnp.dot(normed.reshape(count * span, width), w_qkv, preferred_element_typ...  6.92 us

commit v1 on v0

v1 whole, which is shorter than its diff:
```python
import math

import jax
import jax.numpy as jnp
from jax import lax
from jax.experimental import pallas as pl
from jax.experimental.pallas import tpu as pltpu
from jax.sharding import PartitionSpec as P

MESH = pl.DeviceIdType.MESH
BF16 = jnp.bfloat16
F32 = jnp.float32

HEADS = 16
WIN = 8
D = 512
FF = 2048
HEAD = D // HEADS
SPAN = WIN * WIN
HALVES = 2
GROUP = 4
ROWS = GROUP * SPAN
ZN = 8
LONS = 8
LANES = 128
QUAD = LANES // HEAD
SCALE = math.log2(math.e) / math.sqrt(HEAD)


def norm(x, gain):
    mean = jnp.mean(x, axis=-1, keepdims=True)
    centred = x - mean
    spread = jnp.mean(centred * centred, axis=-1, keepdims=True)
    return (centred * lax.rsqrt(spread + 1e-05) * gain).astype(BF16)


def head_masks():
    lane = lax.broadcasted_iota(jnp.int32, (SPAN, LANES), 1)
    return [(lane >= h * HEAD) & (lane < (h + 1) * HEAD) for h in range(QUAD)]


def attend(load, gain, w_qkv, w_out, q_s, k_s, v_s, mixed_s):
    normed = norm(load(), gain[...])
    q_s[...] = (jnp.dot(normed, w_qkv[:, :D], preferred_element_type=F32) * SCALE).astype(BF16)
    k_s[...] = jnp.dot(normed, w_qkv[:, D : 2 * D], preferred_element_type=F32).astype(BF16)
    v_s[...] = jnp.dot(normed, w_qkv[:, 2 * D :], preferred_element_type=F32).astype(BF16)
    masks = head_masks()
    for w in range(GROUP):
        rows = slice(w * SPAN, (w + 1) * SPAN)
        for g in range(HEADS // QUAD):
            cols = slice(g * LANES, (g + 1) * LANES)
            q = q_s[rows, cols]
            diagonal = jnp.concatenate([jnp.where(m, q, jnp.zeros_like(q)) for m in masks], axis=0)
            scores = lax.dot_general(
                k_s[rows, cols], diagonal, (((1,), (1,)), ((), ())), preferred_element_type=F32
            )
            probs = jnp.exp2(scores - jnp.max(scores, axis=0, keepdims=True))
            probs = (probs * (1.0 / jnp.sum(probs, axis=0, keepdims=True))).astype(BF16)
            mixed = lax.dot_general(
                probs, v_s[rows, cols], (((0,), (0,)), ((), ())), preferred_element_type=F32
            )
            kept = mixed[(QUAD - 1) * SPAN :]
            for h in range(QUAD - 1):
                kept = jnp.where(masks[h], mixed[h * SPAN : (h + 1) * SPAN], kept)
            mixed_s[rows, cols] = kept.astype(BF16)
    return load() + jnp.dot(mixed_s[...], w_out[...], preferred_element_type=F32)


def kernel(
    tokens, block_gain, block_qkv, block_out, grid_gain, grid_qkv, grid_out, mlp_gain, w_up, w_down,
    out,
    x_s, g1, wq1, wo1, g2, wq2, wo2, g3, wu, wd,
    q_s, k_s, v_s, mixed_s, xf, yf,
    send_a, recv_a, send_b, recv_b, out_s,
    load_sem, out_sem, sa, ra, sb, rb,
):
    lat = lax.axis_index("lat")
    lon = lax.axis_index("lon")
    z = lat // 2
    core = lax.rem(lat, 2)
    y = lax.rem(lon, 4)
    xh = lon // 4

    def peer(pz, plon):
        return {"lat": pz * 2 + core, "lon": plon}

    def loads(half):
        return pltpu.make_async_copy(
            tokens.at[pl.ds(half * WIN, WIN)], x_s.at[pl.ds(half * WIN, WIN)], load_sem.at[half]
        )

    weights = [
        pltpu.make_async_copy(src, dst, load_sem.at[HALVES + i])
        for i, (src, dst) in enumerate([
            (block_gain, g1), (block_qkv, wq1), (block_out, wo1),
            (grid_gain, g2), (grid_qkv, wq2), (grid_out, wo2),
            (mlp_gain, g3), (w_up, wu), (w_down, wd),
        ])
    ]
    loads(0).start()
    for copy in weights[:3]:
        copy.start()
    loads(1).start()
    for copy in weights[3:]:
        copy.start()

    def step_of(i):
        return ((i + 1) // 2) * (2 * lax.rem(i, 2) - 1)

    barrier = pltpu.get_barrier_semaphore()

    def greet(i, carry):
        pz = lax.rem(z + step_of(lax.rem(i, ZN)) + ZN, ZN)
        plon = lax.rem(lon + i // ZN, LONS)

        @pl.when(i != 0)
        def _():
            pl.semaphore_signal(barrier, inc=1, device_id=peer(pz, plon), device_id_type=MESH)

        return carry

    lax.fori_loop(0, ZN * LONS, greet, 0)

    mine = z * LONS + lon

    def send(src, dst, send_sem, recv_sem, pz, plon):
        local = (pz == z) & (plon == lon)

        @pl.when(local)
        def _():
            pltpu.make_async_copy(src, dst, recv_sem).start()

        @pl.when(jnp.logical_not(local))
        def _():
            pltpu.make_async_remote_copy(
                src_ref=src, dst_ref=dst, send_sem=send_sem, recv_sem=recv_sem,
                device_id=peer(pz, plon), device_id_type=MESH,
            ).start()

    first = lax.rem(z + xh + y, 2)

    def block_phase(s, carry):
        half = s // 2
        side = lax.rem(s + first, 2)

        @pl.when(s == 0)
        def _():
            loads(0).wait()
            for copy in weights[:3]:
                copy.wait()

        @pl.when(s == 2)
        def _():
            loads(1).wait()

        def load():
            tile = x_s[pl.ds(half * WIN, WIN), pl.ds(pl.multiple_of(side * 32, 32), 32), :].astype(F32)
            return jnp.concatenate(
                [tile[:, w * WIN : (w + 1) * WIN, :].reshape(SPAN, D) for w in range(GROUP)], axis=0
            )

        result = attend(load, g1, wq1, wo1, q_s, k_s, v_s, mixed_s)
        for w in range(GROUP):
            part = result[w * SPAN : (w + 1) * SPAN].reshape(WIN, WIN, D)
            for r in range(WIN):
                send_a[(half * ZN + r) * LONS + side * GROUP + w] = part[r].astype(BF16)

        @pl.when(s == 0)
        def _():
            pl.semaphore_wait(barrier, ZN * LONS - 1)

        def sends(i, carry):
            pz = lax.rem(z + step_of(lax.rem(i, ZN)) + ZN, ZN)
            plon = side * GROUP + lax.rem(y + i // ZN, GROUP)
            send(
                send_a.at[pl.ds((half * ZN + pz) * LONS + plon, 1)],
                recv_a.at[pl.ds(half * ZN * LONS + mine, 1)],
                sa, ra.at[half], pz, plon,
            )
            return carry

        lax.fori_loop(0, ZN * GROUP, sends, 0)
        return carry

    lax.fori_loop(0, 2 * HALVES, block_phase, 0)

    for copy in weights[3:6]:
        copy.wait()

    def grid_phase(half, carry):
        arrived = recv_a.at[pl.ds(half * ZN * LONS, ZN * LONS)]
        pltpu.make_async_copy(arrived, arrived, ra.at[half]).wait()
        for c in range(D // LANES):
            cols = slice(c * LANES, (c + 1) * LANES)
            xf[c] = arrived[:, :, cols].astype(F32).reshape(ZN * LONS * WIN, LANES)

        def four(j, carry):
            def load():
                return jnp.concatenate(
                    [
                        jnp.concatenate(
                            [xf[c, pl.ds(j * GROUP + w, SPAN, stride=WIN), :] for c in range(D // LANES)],
                            axis=1,
                        )
                        for w in range(GROUP)
                    ],
                    axis=0,
                )

            result = attend(load, g2, wq2, wo2, q_s, k_s, v_s, mixed_s)
            for w in range(GROUP):
                for c in range(D // LANES):
                    yf[c, pl.ds(j * GROUP + w, SPAN, stride=WIN), :] = result[
                        w * SPAN : (w + 1) * SPAN, c * LANES : (c + 1) * LANES
                    ]
            return carry

        lax.fori_loop(0, 2, four, 0)
        for c in range(D // LANES):
            send_b[pl.ds(half * ZN * LONS, ZN * LONS), :, c * LANES : (c + 1) * LANES] = (
                yf[c].reshape(ZN * LONS, WIN, LANES).astype(BF16)
            )

        def sends(i, carry):
            pz = lax.rem(z + step_of(lax.rem(i, ZN)) + ZN, ZN)
            plon = lax.rem(lon + i // ZN, LONS)
            send(
                send_b.at[pl.ds((half * ZN + pz) * LONS + plon, 1)],
                recv_b.at[pl.ds(half * ZN * LONS + mine, 1)],
                sb, rb.at[half], pz, plon,
            )
            return carry

        lax.fori_loop(0, ZN * LONS, sends, 0)
        return carry

    lax.fori_loop(0, HALVES, grid_phase, 0)

    for copy in weights[6:]:
        copy.wait()

    per = ROWS // (LONS * WIN)

    def outs(t):
        return pltpu.make_async_copy(
            out_s.at[pl.ds(t * per, per)], out.at[pl.ds(t * per, per)], out_sem.at[t]
        )

    def mlp_phase(t, carry):
        half = t // 2

        @pl.when(lax.rem(t, 2) == 0)
        def _():
            arrived = recv_b.at[pl.ds(half * ZN * LONS, ZN * LONS)]
            pltpu.make_async_copy(arrived, arrived, rb.at[half]).wait()

        def load():
            return recv_b[pl.ds(t * per * LONS, per * LONS)].astype(F32).reshape(ROWS, D)

        normed = norm(load(), g3[...])
        total = load()
        for f in range(FF // D):
            cols = slice(f * D, (f + 1) * D)
            hidden = jax.nn.gelu(
                jnp.dot(normed, wu[:, cols], preferred_element_type=F32), approximate=True
            ).astype(BF16)
            total = total + jnp.dot(hidden, wd[cols, :], preferred_element_type=F32)
        out_s[pl.ds(t * per, per)] = total.astype(BF16).reshape(per, LONS * WIN, D)
        outs(t).start()
        return carry

    lax.fori_loop(0, 2 * HALVES, mlp_phase, 0)

    for t in range(2 * HALVES):
        outs(t).wait()
    gone = send_a.at[pl.ds(0, ZN * LONS * HALVES - HALVES)]
    pltpu.make_async_copy(gone, gone, sa).wait()
    gone = send_b.at[pl.ds(0, ZN * LONS * HALVES - HALVES)]
    pltpu.make_async_copy(gone, gone, sb).wait()


def shards(
    tokens, block_gain, block_qkv, block_out, grid_gain, grid_qkv, grid_out, mlp_gain, w_up, w_down
):
    rows, cols, width = tokens.shape
    slabs = HALVES * ZN * LONS
    any_spec = pl.BlockSpec(memory_space=pl.ANY)
    vmem = pltpu.VMEM
    return pl.pallas_call(
        kernel,
        out_shape=jax.ShapeDtypeStruct(tokens.shape, BF16),
        in_specs=[any_spec] * 10,
        out_specs=any_spec,
        scratch_shapes=[
            vmem((rows, cols, D), BF16),
            vmem((1, D), F32), vmem((D, 3 * D), BF16), vmem((D, D), BF16),
            vmem((1, D), F32), vmem((D, 3 * D), BF16), vmem((D, D), BF16),
            vmem((1, D), F32), vmem((D, FF), BF16), vmem((FF, D), BF16),
            vmem((ROWS, D), BF16), vmem((ROWS, D), BF16), vmem((ROWS, D), BF16), vmem((ROWS, D), BF16),
            vmem((D // LANES, ZN * LONS * WIN, LANES), F32), vmem((D // LANES, ZN * LONS * WIN, LANES), F32),
            vmem((slabs, WIN, D), BF16), vmem((slabs, WIN, D), BF16),
            vmem((slabs, WIN, D), BF16), vmem((slabs, WIN, D), BF16),
            vmem((rows, cols, D), BF16),
            pltpu.SemaphoreType.DMA((HALVES + 9,)),
            pltpu.SemaphoreType.DMA((2 * HALVES,)),
            pltpu.SemaphoreType.DMA,
            pltpu.SemaphoreType.DMA((HALVES,)),
            pltpu.SemaphoreType.DMA,
            pltpu.SemaphoreType.DMA((HALVES,)),
        ],
        compiler_params=pltpu.CompilerParams(
            collective_id=0, has_side_effects=True, vmem_limit_bytes=48 << 20
        ),
    )(
        tokens, block_gain.reshape(1, D), block_qkv, block_out, grid_gain.reshape(1, D), grid_qkv, grid_out,
        mlp_gain.reshape(1, D), w_up, w_down,
    )


def solution(mesh):
    in_specs = (P(("samp", "lat"), "lon", None), P(), P(), P(), P(), P(), P(), P(), P(), P())
    out_specs = P(("samp", "lat"), "lon", None)
    return jax.shard_map(shards, mesh=mesh, in_specs=in_specs, out_specs=out_specs, check_vma=False)
```

time: 198 us -> 73.6 us (0.37)
  blocking collectives: 83.7 us -> 0 us
  Pallas kernels: 0 us -> 64.4 us
  local copies, waits for them, and re-layouts: 49.4 us -> 7.73 us
  other arithmetic: 39.6 us -> 0 us
  matrix products: 23 us -> 0 us
    all_to_all x2 -> x0, blocking collectives: 83.7 us -> none  [the longest x1 46.2 us: send_out(): lax.all_to_all(pieces, ('lat', 'lon'), split_axis=0, concat_axis=1, tiled...]
    pallas_call x0 -> x1, Pallas kernels: none -> 64.4 us  [shards(): pl.pallas_call(kernel, out_shape=jax.ShapeDtypeStruct(tokens.shape, BF16)...]
    sub x2 -> x0, other arithmetic: 24.3 us -> none  [window_attention(): weights_soft = jax.nn.softmax(scores, axis=-1).astype(jnp.bfloat16)]
    dot_general x9 -> x0, matrix products: 23 us -> none  [the longest x1 7.66 us: feed_forward(): jnp.dot(hidden, w_down, preferred_element_type=jnp.float32)]
    reshape x4 -> x0, local copies, waits for them, and re-layouts: 19.1 us -> none  [the longest x2 18.4 us: window_attention(): projected.astype(jnp.bfloat16).reshape(count, span, 3, HEADS, head_size)]
    convert_element_type x5 -> x0, local copies, waits for them, and re-layouts: 17.1 us -> none  [the longest x2 9.46 us: window_attention(): projected.astype(jnp.bfloat16).reshape(count, span, 3, HEADS, head_size)]
    convert_element_type x6 -> x0, other arithmetic: 10.5 us -> none  [the longest x2 6.05 us: feed_forward(): return (tile.astype(jnp.float32) + result).astype(jnp.bfloat16)]
    slice x2 -> x0, local copies, waits for them, and re-layouts: 8.91 us -> none  [window_attention(): values_all = projected[:, :, 2]]
where the time goes in v1:
time: 73.6 us; the launch traced here: 72.2 us
  Pallas kernels  64.4 us (88%)
  local copies, waits for them, and re-layouts  7.73 us (11%)
    pallas_call x1, Pallas kernels, shards(): pl.pallas_call(kernel, out_shape=jax.ShapeDtypeStruct(tokens.shape, BF16)...  64.4 us
    unnamed x15, local copies, waits for them, and re-layouts  7.73 us

profile of v1, /device:TPU:32, one launch (start us, length us, event | category | flops | bytes accessed | tf_op | source)
XLA Modules:
  0.0 72.2 jit_solution(15084668610974482413)
XLA Ops:
  0.0 0.0 copy-start
  0.0 1.4 %copy-done = bf16[512,1536]{1,0:T(8,128)(2,1)S(1)} copy-done((bf16[512,1536]{1,0:T(8,128)(2,1)S(1)}, bf16[512,1536]{1,0:T(8,128)(2,1)}, u32[]{:S(2)}) %copy-start) | copy-done | bytes 1572888
  1.4 0.0 copy-start.1
  1.4 1.2 %copy-done.1 = bf16[16,64,512]{2,1,0:T(8,128)(2,1)S(1)} copy-done((bf16[16,64,512]{2,1,0:T(8,128)(2,1)S(1)}, bf16[16,64,512]{2,1,0:T(8,128)(2,1)}, u32[]{:S(2)}) %copy-start.1) | copy-done | bytes 1048600
  2.6 0.0 copy-start.2
  2.6 1.0 %copy-done.2 = bf16[512,512]{1,0:T(8,128)(2,1)S(1)} copy-done((bf16[512,512]{1,0:T(8,128)(2,1)S(1)}, bf16[512,512]{1,0:T(8,128)(2,1)}, u32[]{:S(2)}) %copy-start.2) | copy-done | bytes 524312
  3.7 0.0 copy-start.3
  3.7 1.0 %copy-done.3 = bf16[512,512]{1,0:T(8,128)(2,1)S(1)} copy-done((bf16[512,512]{1,0:T(8,128)(2,1)S(1)}, bf16[512,512]{1,0:T(8,128)(2,1)}, u32[]{:S(2)}) %copy-start.3) | copy-done | bytes 524312
  4.7 0.0 copy-start.4
  4.7 0.7 copy-done.4
  5.4 0.0 copy-start.5
  5.4 0.7 copy-done.5
  6.1 0.0 copy-start.6
  6.1 0.7 copy-done.6
  6.8 64.4 %shard_map.100 = bf16[16,64,512]{2,1,0:T(8,128)(2,1)S(1)} custom-call(bf16[16,64,512]{2,1,0:T(8,128)(2,1)S(1)} %copy-done.1, f32[1,512]{1,0:T(1,128)S(1)} %bitcast.3, bf16[512,1536]{1,0:T(8,128)(2,1)S(1)} %copy-done, bf16[512,512]{1,0:T(8,128)(2,1)S(1)} %copy-done.2, f32[1,512]{1,0:T(1,128)S(1)} %bitcast.4, bf16[512,1536]{1,0:T(8,128)(2,1)} %grid_qkv.1, ...), custom_call_target="tpu_custom_call" | custom-call | tf_op jit(solution)/shard_map/pallas_call | solution.py:289
  71.2 1.0 %copy.12 = bf16[16,64,512]{2,1,0:T(8,128)(2,1)} copy(bf16[16,64,512]{2,1,0:T(8,128)(2,1)S(1)} %shard_map.100) | data formatting | bytes 2097152
Async XLA Ops:
  0.0 1.4 %copy-start = (bf16[512,1536]{1,0:T(8,128)(2,1)S(1)}, bf16[512,1536]{1,0:T(8,128)(2,1)}, u32[]{:S(2)}) copy-start(bf16[512,1536]{1,0:T(8,128)(2,1)} %block_qkv.1) | copy-start | bytes 4718596
  1.4 1.2 %copy-start.1 = (bf16[16,64,512]{2,1,0:T(8,128)(2,1)S(1)}, bf16[16,64,512]{2,1,0:T(8,128)(2,1)}, u32[]{:S(2)}) copy-start(bf16[16,64,512]{2,1,0:T(8,128)(2,1)} %tokens.1) | copy-start | bytes 3145732
  2.6 1.0 %copy-start.2 = (bf16[512,512]{1,0:T(8,128)(2,1)S(1)}, bf16[512,512]{1,0:T(8,128)(2,1)}, u32[]{:S(2)}) copy-start(bf16[512,512]{1,0:T(8,128)(2,1)} %block_out.1) | copy-start | bytes 1572868
  3.7 1.0 %copy-start.3 = (bf16[512,512]{1,0:T(8,128)(2,1)S(1)}, bf16[512,512]{1,0:T(8,128)(2,1)}, u32[]{:S(2)}) copy-start(bf16[512,512]{1,0:T(8,128)(2,1)} %grid_out.1) | copy-start | bytes 1572868
  4.7 0.7 copy-start.4
  5.4 0.7 copy-start.5
  6.1 0.7 copy-start.6

commit v2 on v1

v2 whole, which is shorter than its diff:
```python
import math

import jax
import jax.numpy as jnp
from jax import lax
from jax.experimental import pallas as pl
from jax.experimental.pallas import tpu as pltpu
from jax.sharding import PartitionSpec as P

MESH = pl.DeviceIdType.MESH
BF16 = jnp.bfloat16
F32 = jnp.float32

HEADS = 16
WIN = 8
D = 512
FF = 2048
HEAD = D // HEADS
SPAN = WIN * WIN
HALVES = 2
GROUP = 4
ROWS = GROUP * SPAN
QUARTERS = 4
ZN = 8
ZHALF = 4
LONS = 8
SLABS = ZN * LONS
PAIR = 2
STEPS = LONS // PAIR
Z_OFFSETS = (1, -1, 2, -2, 3, -3, 4, 0)
LANES = 128
QUAD = LANES // HEAD
SCALE = math.log2(math.e) / math.sqrt(HEAD)


def norm(x, gain):
    mean = jnp.mean(x, axis=-1, keepdims=True)
    centred = x - mean
    spread = jnp.mean(centred * centred, axis=-1, keepdims=True)
    return (centred * lax.rsqrt(spread + 1e-05) * gain).astype(BF16)


def head_masks():
    lane = lax.broadcasted_iota(jnp.int32, (SPAN, LANES), 1)
    return [(lane >= h * HEAD) & (lane < (h + 1) * HEAD) for h in range(QUAD)]


def attend(load, gain, w_qkv, w_out, q_s, k_s, v_s, mixed_s):
    normed = norm(load(), gain[...])
    q_s[...] = (jnp.dot(normed, w_qkv[:, :D], preferred_element_type=F32) * SCALE).astype(BF16)
    k_s[...] = jnp.dot(normed, w_qkv[:, D : 2 * D], preferred_element_type=F32).astype(BF16)
    v_s[...] = jnp.dot(normed, w_qkv[:, 2 * D :], preferred_element_type=F32).astype(BF16)
    masks = head_masks()
    for w in range(GROUP):
        rows = slice(w * SPAN, (w + 1) * SPAN)
        for g in range(HEADS // QUAD):
            cols = slice(g * LANES, (g + 1) * LANES)
            q = q_s[rows, cols]
            diagonal = jnp.concatenate([jnp.where(m, q, jnp.zeros_like(q)) for m in masks], axis=0)
            scores = lax.dot_general(
                k_s[rows, cols], diagonal, (((1,), (1,)), ((), ())), preferred_element_type=F32
            )
            probs = jnp.exp2(scores - jnp.max(scores, axis=0, keepdims=True))
            probs = (probs * (1.0 / jnp.sum(probs, axis=0, keepdims=True))).astype(BF16)
            mixed = lax.dot_general(
                probs, v_s[rows, cols], (((0,), (0,)), ((), ())), preferred_element_type=F32
            )
            kept = mixed[(QUAD - 1) * SPAN :]
            for h in range(QUAD - 1):
                kept = jnp.where(masks[h], mixed[h * SPAN : (h + 1) * SPAN], kept)
            mixed_s[rows, cols] = kept.astype(BF16)
    return load() + jnp.dot(mixed_s[...], w_out[...], preferred_element_type=F32)


def kernel(
    tokens, block_gain, block_qkv, block_out, grid_gain, grid_qkv, grid_out, mlp_gain, w_up, w_down,
    out,
    x_s, g1, wq1, wo1, g2, wq2, wo2, g3, wu, wd,
    q_s, k_s, v_s, mixed_s, xf, yf,
    send_a, recv_a, send_b, recv_b, out_s,
    load_sem, out_sem, sa, ra, sb, rb,
):
    lat = lax.axis_index("lat")
    lon = lax.axis_index("lon")
    z = lat // 2
    core = lax.rem(lat, 2)

    def peer(pz, plon):
        return {"lat": pz * 2 + core, "lon": plon}

    def quarter_load(q):
        part = (pl.ds(q // 2 * WIN, WIN), pl.ds(q % 2 * GROUP * WIN, GROUP * WIN))
        return pltpu.make_async_copy(tokens.at[part], x_s.at[part], load_sem.at[q])

    def around(off):
        return lax.rem(z + off + ZN, ZN)

    barrier = pltpu.get_barrier_semaphore()

    for b in range(LONS):
        plon = lax.rem(lon + b, LONS)
        for off in Z_OFFSETS:
            if b or off:
                pl.semaphore_signal(
                    barrier, inc=1, device_id=peer(around(off), plon), device_id_type=MESH
                )

    weights = [
        pltpu.make_async_copy(src, dst, load_sem.at[QUARTERS + i])
        for i, (src, dst) in enumerate([
            (block_gain, g1), (block_qkv, wq1), (block_out, wo1),
            (grid_gain, g2), (grid_qkv, wq2), (grid_out, wo2),
            (mlp_gain, g3), (w_up, wu), (w_down, wd),
        ])
    ]
    quarter_load(0).start()
    for copy in weights[:3]:
        copy.start()
    for q in range(1, QUARTERS):
        quarter_load(q).start()
    for copy in weights[3:]:
        copy.start()

    mine = z * LONS + lon

    def push(src, dst, send_sem, recv_sem, pz, plon):
        pltpu.make_async_remote_copy(
            src_ref=src, dst_ref=dst, send_sem=send_sem, recv_sem=recv_sem,
            device_id=peer(pz, plon), device_id_type=MESH,
        ).start()

    def push_or_keep(local, src, dst, send_sem, recv_sem, pz, plon):
        @pl.when(local)
        def _():
            pltpu.make_async_copy(src, dst, recv_sem).start()

        @pl.when(jnp.logical_not(local))
        def _():
            push(src, dst, send_sem, recv_sem, pz, plon)

    def arrived(ref, sem):
        pltpu.make_async_copy(ref, ref, sem).wait()

    parity = lax.rem(z, 2)

    def block_phase(q, carry):
        half = q // 2
        side = lax.rem(q, 2)

        @pl.when(q == 0)
        def _():
            for copy in weights[:3]:
                copy.wait()

        for i in range(QUARTERS):
            @pl.when(q == i)
            def _():
                quarter_load(i).wait()

        def load():
            tile = x_s[pl.ds(half * WIN, WIN), pl.ds(pl.multiple_of(side * 32, 32), 32), :].astype(F32)
            return jnp.concatenate(
                [tile[:, w * WIN : (w + 1) * WIN, :].reshape(SPAN, D) for w in range(GROUP)], axis=0
            )

        result = attend(load, g1, wq1, wo1, q_s, k_s, v_s, mixed_s)
        for w in range(GROUP):
            part = result[w * SPAN : (w + 1) * SPAN].reshape(WIN, WIN, D)
            for r in range(WIN):
                send_a[(q * LONS + r) * ZHALF + w] = part[r].astype(BF16)

        @pl.when(q == 0)
        def _():
            pl.semaphore_wait(barrier, SLABS - 1)

        def sends(b, carry):
            plon = lax.rem(lon + b, LONS)
            for i in (1, 3, 2, 0):
                w = lax.rem(z // 2 + i, ZHALF)
                src = send_a.at[pl.ds((q * LONS + plon) * ZHALF + w, 1)]
                dst = recv_a.at[pl.ds(half * SLABS + mine, 1)]
                if i:
                    push(src, dst, sa, ra.at[half], 2 * w + side, plon)
                else:
                    push_or_keep((b == 0) & (side == parity), src, dst, sa, ra.at[half], 2 * w + side, plon)
            return carry

        lax.fori_loop(0, LONS, sends, 0)
        return carry

    lax.fori_loop(0, QUARTERS, block_phase, 0)

    for copy in weights[3:6]:
        copy.wait()

    def grid_phase(half, carry):
        slabs = pl.ds(half * SLABS, SLABS)
        arrived(recv_a.at[slabs], ra.at[half])
        for c in range(D // LANES):
            cols = slice(c * LANES, (c + 1) * LANES)
            xf[c] = recv_a[slabs, :, cols].astype(F32).reshape(SLABS * WIN, LANES)

        def four(j, carry):
            def load():
                return jnp.concatenate(
                    [
                        jnp.concatenate(
                            [xf[c, pl.ds(j * GROUP + w, SPAN, stride=WIN), :] for c in range(D // LANES)],
                            axis=1,
                        )
                        for w in range(GROUP)
                    ],
                    axis=0,
                )

            result = attend(load, g2, wq2, wo2, q_s, k_s, v_s, mixed_s)
            for w in range(GROUP):
                for c in range(D // LANES):
                    yf[c, pl.ds(j * GROUP + w, SPAN, stride=WIN), :] = result[
                        w * SPAN : (w + 1) * SPAN, c * LANES : (c + 1) * LANES
                    ]
            return carry

        lax.fori_loop(0, 2, four, 0)
        for c in range(D // LANES):
            send_b[slabs, :, c * LANES : (c + 1) * LANES] = (
                yf[c].reshape(SLABS, WIN, LANES).astype(BF16)
            )

        def sends(b, carry):
            plon = lax.rem(lon + b, LONS)
            dst = recv_b.at[pl.ds((half * LONS + b) * ZN + parity * ZHALF + z // 2, 1)]
            sem = rb.at[half * STEPS + b // PAIR]
            for off in Z_OFFSETS:
                pz = around(off)
                src = send_b.at[pl.ds(half * SLABS + pz * LONS + plon, 1)]
                if off:
                    push(src, dst, sb, sem, pz, plon)
                else:
                    push_or_keep(b == 0, src, dst, sb, sem, pz, plon)
            return carry

        lax.fori_loop(0, LONS, sends, 0)
        return carry

    lax.fori_loop(0, HALVES, grid_phase, 0)

    for copy in weights[6:]:
        copy.wait()

    def outs(t, i):
        row = t // STEPS * WIN + lax.rem(lon - lax.rem(t, STEPS) * PAIR - i + LONS, LONS)
        return pltpu.make_async_copy(out_s.at[t * PAIR + i], out.at[row], out_sem.at[t])

    def mlp_phase(t, carry):
        slabs = pl.ds(t * (PAIR * ZN), PAIR * ZN)
        arrived(recv_b.at[slabs], rb.at[t])

        def load():
            return recv_b[slabs].astype(F32).reshape(PAIR * SPAN, D)

        normed = norm(load(), g3[...])
        total = load()
        for f in range(FF // D):
            cols = slice(f * D, (f + 1) * D)
            hidden = jax.nn.gelu(
                jnp.dot(normed, wu[:, cols], preferred_element_type=F32), approximate=True
            ).astype(BF16)
            total = total + jnp.dot(hidden, wd[cols, :], preferred_element_type=F32)
        out_s[pl.ds(t * PAIR, PAIR)] = total.astype(BF16).reshape(PAIR, SPAN, D)
        for i in range(PAIR):
            outs(t, i).start()
        return carry

    lax.fori_loop(0, HALVES * STEPS, mlp_phase, 0)

    for t in range(HALVES * STEPS):
        arrived(out_s.at[pl.ds(t * PAIR, PAIR)], out_sem.at[t])
    gone = send_a.at[pl.ds(0, HALVES * (SLABS - 1))]
    arrived(gone, sa)
    arrived(gone, sb)


def shards(
    tokens, block_gain, block_qkv, block_out, grid_gain, grid_qkv, grid_out, mlp_gain, w_up, w_down
):
    rows, cols, width = tokens.shape
    slabs = HALVES * SLABS
    any_spec = pl.BlockSpec(memory_space=pl.ANY)
    vmem = pltpu.VMEM
    return pl.pallas_call(
        kernel,
        out_shape=jax.ShapeDtypeStruct(tokens.shape, BF16),
        in_specs=[any_spec] * 10,
        out_specs=any_spec,
        scratch_shapes=[
            vmem((rows, cols, D), BF16),
            vmem((1, D), F32), vmem((D, 3 * D), BF16), vmem((D, D), BF16),
            vmem((1, D), F32), vmem((D, 3 * D), BF16), vmem((D, D), BF16),
            vmem((1, D), F32), vmem((D, FF), BF16), vmem((FF, D), BF16),
            vmem((ROWS, D), BF16), vmem((ROWS, D), BF16), vmem((ROWS, D), BF16), vmem((ROWS, D), BF16),
            vmem((D // LANES, SLABS * WIN, LANES), F32), vmem((D // LANES, SLABS * WIN, LANES), F32),
            vmem((slabs, WIN, D), BF16), vmem((slabs, WIN, D), BF16),
            vmem((slabs, WIN, D), BF16), vmem((slabs, WIN, D), BF16),
            vmem((rows, cols, D), BF16),
            pltpu.SemaphoreType.DMA((QUARTERS + 9,)),
            pltpu.SemaphoreType.DMA((HALVES * STEPS,)),
            pltpu.SemaphoreType.DMA,
            pltpu.SemaphoreType.DMA((HALVES,)),
            pltpu.SemaphoreType.DMA,
            pltpu.SemaphoreType.DMA((HALVES * STEPS,)),
        ],
        compiler_params=pltpu.CompilerParams(
            collective_id=0, has_side_effects=True, vmem_limit_bytes=48 << 20
        ),
    )(*[pltpu.with_memory_space_constraint(a, pltpu.HBM) for a in (
        tokens, block_gain.reshape(1, D), block_qkv, block_out, grid_gain.reshape(1, D), grid_qkv, grid_out,
        mlp_gain.reshape(1, D), w_up, w_down,
    )])


def solution(mesh):
    in_specs = (P(("samp", "lat"), "lon", None), P(), P(), P(), P(), P(), P(), P(), P(), P())
    out_specs = P(("samp", "lat"), "lon", None)
    return jax.shard_map(shards, mesh=mesh, in_specs=in_specs, out_specs=out_specs, check_vma=False)
```

time: 73.6 us -> 63.3 us (0.86); the launches traced: 72.2 us -> 63 us
  local copies, waits for them, and re-layouts: 7.73 us -> 0.97 us
  Pallas kernels: 64.4 us -> 62 us
    unnamed x15 -> x1, local copies, waits for them, and re-layouts: 7.73 us -> 0.97 us
    pallas_call x1, Pallas kernels: 64.4 us -> 62 us  [shards(): pl.pallas_call(kernel, out_shape=jax.ShapeDtypeStruct(tokens.shape, BF16)...]
where the time goes in v2:
time: 63.3 us; the launch traced here: 63 us
  Pallas kernels  62 us (98%)
  local copies, waits for them, and re-layouts  0.97 us (2%)
    pallas_call x1, Pallas kernels, shards(): pl.pallas_call(kernel, out_shape=jax.ShapeDtypeStruct(tokens.shape, BF16)...  62 us

profile of v2, /device:TPU:32, one launch (start us, length us, event | category | flops | bytes accessed | tf_op | source)
XLA Modules:
  0.0 63.0 jit_solution(13426645385976514529)
XLA Ops:
  0.0 62.0 %shard_map.100 = bf16[16,64,512]{2,1,0:T(8,128)(2,1)S(1)} custom-call(bf16[16,64,512]{2,1,0:T(8,128)(2,1)} %tokens.1, f32[1,512]{1,0:T(1,128)} %bitcast.3, bf16[512,1536]{1,0:T(8,128)(2,1)} %block_qkv.1, bf16[512,512]{1,0:T(8,128)(2,1)} %block_out.1, f32[1,512]{1,0:T(1,128)} %bitcast.4, bf16[512,1536]{1,0:T(8,128)(2,1)} %grid_qkv.1, ...), custom_call_target="tpu_custom_call" | custom-call | tf_op jit(solution)/shard_map/pallas_call | solution.py:291
  62.1 1.0 %copy.12 = bf16[16,64,512]{2,1,0:T(8,128)(2,1)} copy(bf16[16,64,512]{2,1,0:T(8,128)(2,1)S(1)} %shard_map.100) | data formatting | bytes 2097152

commit v3 on v2

--- a/solution.py
+++ b/solution.py
@@ -25,8 +25,6 @@
 ZHALF = 4
 LONS = 8
 SLABS = ZN * LONS
-PAIR = 2
-STEPS = LONS // PAIR
 Z_OFFSETS = (1, -1, 2, -2, 3, -3, 4, 0)
 LANES = 128
 QUAD = LANES // HEAD
@@ -77,8 +75,8 @@
     out,
     x_s, g1, wq1, wo1, g2, wq2, wo2, g3, wu, wd,
     q_s, k_s, v_s, mixed_s, xf, yf,
-    send_a, recv_a, send_b, recv_b, out_s,
-    load_sem, out_sem, sa, ra, sb, rb,
+    send_a, recv_a, send_b,
+    load_sem, sa, ra, sb, rb,
 ):
     lat = lax.axis_index("lat")
     lon = lax.axis_index("lon")
@@ -121,8 +119,6 @@
     for copy in weights[3:]:
         copy.start()
 
-    mine = z * LONS + lon
-
     def push(src, dst, send_sem, recv_sem, pz, plon):
         pltpu.make_async_remote_copy(
             src_ref=src, dst_ref=dst, send_sem=send_sem, recv_sem=recv_sem,
@@ -178,7 +174,7 @@
             for i in (1, 3, 2, 0):
                 w = lax.rem(z // 2 + i, ZHALF)
                 src = send_a.at[pl.ds((q * LONS + plon) * ZHALF + w, 1)]
-                dst = recv_a.at[pl.ds(half * SLABS + mine, 1)]
+                dst = recv_a.at[pl.ds(half * SLABS + b * ZN + z, 1)]
                 if i:
                     push(src, dst, sa, ra.at[half], 2 * w + side, plon)
                 else:
@@ -190,7 +186,7 @@
 
     lax.fori_loop(0, QUARTERS, block_phase, 0)
 
-    for copy in weights[3:6]:
+    for copy in weights[3:]:
         copy.wait()
 
     def grid_phase(half, carry):
@@ -222,60 +218,47 @@
             return carry
 
         lax.fori_loop(0, 2, four, 0)
-        for c in range(D // LANES):
-            send_b[slabs, :, c * LANES : (c + 1) * LANES] = (
-                yf[c].reshape(SLABS, WIN, LANES).astype(BF16)
+        dst = out.at[pl.ds((half * WIN + lon) * LONS + parity * ZHALF + z // 2, 1)]
+
+        def forward(j, carry):
+            part = pl.ds(pl.multiple_of(j * ROWS, ROWS), ROWS)
+
+            def load():
+                return jnp.concatenate([yf[c, part, :] for c in range(D // LANES)], axis=1).astype(BF16).astype(F32)
+
+            normed = norm(load(), g3[...])
+            total = load()
+            for f in range(FF // D):
+                cols = slice(f * D, (f + 1) * D)
+                hidden = jax.nn.gelu(
+                    jnp.dot(normed, wu[:, cols], preferred_element_type=F32), approximate=True
+                ).astype(BF16)
+                total = total + jnp.dot(hidden, wd[cols, :], preferred_element_type=F32)
+            send_b[pl.ds(half * SLABS + j * (ROWS // WIN), ROWS // WIN)] = (
+                total.astype(BF16).reshape(ROWS // WIN, WIN, D)
             )
 
-        def sends(b, carry):
-            plon = lax.rem(lon + b, LONS)
-            dst = recv_b.at[pl.ds((half * LONS + b) * ZN + parity * ZHALF + z // 2, 1)]
-            sem = rb.at[half * STEPS + b // PAIR]
-            for off in Z_OFFSETS:
-                pz = around(off)
-                src = send_b.at[pl.ds(half * SLABS + pz * LONS + plon, 1)]
-                if off:
-                    push(src, dst, sb, sem, pz, plon)
-                else:
-                    push_or_keep(b == 0, src, dst, sb, sem, pz, plon)
+            def sends(i, carry):
+                b = j * (LONS // 2) + i
+                plon = lax.rem(lon - b + LONS, LONS)
+                for off in Z_OFFSETS:
+                    pz = around(off)
+                    src = send_b.at[pl.ds(half * SLABS + b * ZN + pz, 1)]
+                    if off:
+                        push(src, dst, sb, rb, pz, plon)
+                    else:
+                        push_or_keep(b == 0, src, dst, sb, rb, pz, plon)
+                return carry
+
+            lax.fori_loop(0, LONS // 2, sends, 0)
             return carry
 
-        lax.fori_loop(0, LONS, sends, 0)
+        lax.fori_loop(0, 2, forward, 0)
         return carry
 
     lax.fori_loop(0, HALVES, grid_phase, 0)
 
-    for copy in weights[6:]:
-        copy.wait()
-
-    def outs(t, i):
-        row = t // STEPS * WIN + lax.rem(lon - lax.rem(t, STEPS) * PAIR - i + LONS, LONS)
-        return pltpu.make_async_copy(out_s.at[t * PAIR + i], out.at[row], out_sem.at[t])
-
-    def mlp_phase(t, carry):
-        slabs = pl.ds(t * (PAIR * ZN), PAIR * ZN)
-        arrived(recv_b.at[slabs], rb.at[t])
-
-        def load():
-            return recv_b[slabs].astype(F32).reshape(PAIR * SPAN, D)
-
-        normed = norm(load(), g3[...])
-        total = load()
-        for f in range(FF // D):
-            cols = slice(f * D, (f + 1) * D)
-            hidden = jax.nn.gelu(
-                jnp.dot(normed, wu[:, cols], preferred_element_type=F32), approximate=True
-            ).astype(BF16)
-            total = total + jnp.dot(hidden, wd[cols, :], preferred_element_type=F32)
-        out_s[pl.ds(t * PAIR, PAIR)] = total.astype(BF16).reshape(PAIR, SPAN, D)
-        for i in range(PAIR):
-            outs(t, i).start()
-        return carry
-
-    lax.fori_loop(0, HALVES * STEPS, mlp_phase, 0)
-
-    for t in range(HALVES * STEPS):
-        arrived(out_s.at[pl.ds(t * PAIR, PAIR)], out_sem.at[t])
+    arrived(out, rb)
     gone = send_a.at[pl.ds(0, HALVES * (SLABS - 1))]
     arrived(gone, sa)
     arrived(gone, sb)
@@ -288,9 +271,9 @@
     slabs = HALVES * SLABS
     any_spec = pl.BlockSpec(memory_space=pl.ANY)
     vmem = pltpu.VMEM
-    return pl.pallas_call(
+    result = pl.pallas_call(
         kernel,
-        out_shape=jax.ShapeDtypeStruct(tokens.shape, BF16),
+        out_shape=jax.ShapeDtypeStruct((slabs, WIN, D), BF16),
         in_specs=[any_spec] * 10,
         out_specs=any_spec,
         scratch_shapes=[
@@ -300,15 +283,12 @@
             vmem((1, D), F32), vmem((D, FF), BF16), vmem((FF, D), BF16),
             vmem((ROWS, D), BF16), vmem((ROWS, D), BF16), vmem((ROWS, D), BF16), vmem((ROWS, D), BF16),
             vmem((D // LANES, SLABS * WIN, LANES), F32), vmem((D // LANES, SLABS * WIN, LANES), F32),
-            vmem((slabs, WIN, D), BF16), vmem((slabs, WIN, D), BF16),
-            vmem((slabs, WIN, D), BF16), vmem((slabs, WIN, D), BF16),
-            vmem((rows, cols, D), BF16),
+            vmem((slabs, WIN, D), BF16), vmem((slabs, WIN, D), BF16), vmem((slabs, WIN, D), BF16),
             pltpu.SemaphoreType.DMA((QUARTERS + 9,)),
-            pltpu.SemaphoreType.DMA((HALVES * STEPS,)),
             pltpu.SemaphoreType.DMA,
             pltpu.SemaphoreType.DMA((HALVES,)),
             pltpu.SemaphoreType.DMA,
-            pltpu.SemaphoreType.DMA((HALVES * STEPS,)),
+            pltpu.SemaphoreType.DMA,
         ],
         compiler_params=pltpu.CompilerParams(
             collective_id=0, has_side_effects=True, vmem_limit_bytes=48 << 20
@@ -317,6 +297,7 @@
         tokens, block_gain.reshape(1, D), block_qkv, block_out, grid_gain.reshape(1, D), grid_qkv, grid_out,
         mlp_gain.reshape(1, D), w_up, w_down,
     )])
+    return result.reshape(tokens.shape)
 
 
 def solution(mesh):

time: 63.3 us -> 62.7 us (level)
  no operation moved by 1% of the time
where the time goes in v3:
time: 62.7 us; the launch traced here: 62.5 us
  Pallas kernels  61.5 us (98%)
  local copies, waits for them, and re-layouts  0.97 us (2%)
    pallas_call x1, Pallas kernels, shards(): pl.pallas_call(kernel, out_shape=jax.ShapeDtypeStruct((slabs, WIN, D), BF...  61.5 us

profile of v3, /device:TPU:32, one launch (start us, length us, event | category | flops | bytes accessed | tf_op | source)
XLA Modules:
  0.0 62.5 jit_solution(10332382376176674503)
XLA Ops:
  0.0 61.5 %shard_map.100 = bf16[128,8,512]{2,1,0:T(8,128)(2,1)S(1)} custom-call(bf16[16,64,512]{2,1,0:T(8,128)(2,1)} %tokens.1, f32[1,512]{1,0:T(1,128)} %bitcast.5, bf16[512,1536]{1,0:T(8,128)(2,1)} %block_qkv.1, bf16[512,512]{1,0:T(8,128)(2,1)} %block_out.1, f32[1,512]{1,0:T(1,128)} %bitcast.6, bf16[512,1536]{1,0:T(8,128)(2,1)} %grid_qkv.1, ...), custom_call_target="tpu_custom_call" | custom-call | tf_op jit(solution)/shard_map/pallas_call | solution.py:274
  61.5 1.0 %copy.12 = bf16[16,64,512]{2,1,0:T(8,128)(2,1)} copy(bf16[16,64,512]{2,1,0:T(8,128)(2,1)S(1)} %bitcast.4) | data formatting | bytes 2097152

commit v4 on v3

--- a/solution.py
+++ b/solution.py
@@ -24,8 +24,9 @@
 ZN = 8
 ZHALF = 4
 LONS = 8
+YN = 4
 SLABS = ZN * LONS
-Z_OFFSETS = (1, -1, 2, -2, 3, -3, 4, 0)
+Z_OFFSETS = (4, 3, -3, 2, -2, 1, -1, 0)
 LANES = 128
 QUAD = LANES // HEAD
 SCALE = math.log2(math.e) / math.sqrt(HEAD)
@@ -76,7 +77,7 @@
     x_s, g1, wq1, wo1, g2, wq2, wo2, g3, wu, wd,
     q_s, k_s, v_s, mixed_s, xf, yf,
     send_a, recv_a, send_b,
-    load_sem, sa, ra, sb, rb,
+    load_sem, sa, ra, sb, rb, ready,
 ):
     lat = lax.axis_index("lat")
     lon = lax.axis_index("lon")
@@ -93,15 +94,22 @@
     def around(off):
         return lax.rem(z + off + ZN, ZN)
 
+    def steps_of_y(b):
+        h = b % YN
+        return h + h // 2 - 2 * (h // 3)
+
+    def ahead(b):
+        return lax.rem(lon // YN + b // YN, 2) * YN + lax.rem(lon % YN + steps_of_y(b), YN)
+
+    def behind(b):
+        return lax.rem(lon // YN + b // YN, 2) * YN + lax.rem(lon % YN + YN - steps_of_y(b), YN)
+
     barrier = pltpu.get_barrier_semaphore()
 
-    for b in range(LONS):
-        plon = lax.rem(lon + b, LONS)
-        for off in Z_OFFSETS:
-            if b or off:
-                pl.semaphore_signal(
-                    barrier, inc=1, device_id=peer(around(off), plon), device_id_type=MESH
-                )
+    for off in Z_OFFSETS[:-1]:
+        pl.semaphore_signal(barrier, inc=1, device_id=peer(around(off), lon), device_id_type=MESH)
+    for b in range(1, LONS):
+        pl.semaphore_signal(barrier, inc=1, device_id=peer(z, ahead(b)), device_id_type=MESH)
 
     weights = [
         pltpu.make_async_copy(src, dst, load_sem.at[QUARTERS + i])
@@ -114,10 +122,6 @@
     quarter_load(0).start()
     for copy in weights[:3]:
         copy.start()
-    for q in range(1, QUARTERS):
-        quarter_load(q).start()
-    for copy in weights[3:]:
-        copy.start()
 
     def push(src, dst, send_sem, recv_sem, pz, plon):
         pltpu.make_async_remote_copy(
@@ -167,10 +171,19 @@
 
         @pl.when(q == 0)
         def _():
-            pl.semaphore_wait(barrier, SLABS - 1)
+            pl.semaphore_wait(barrier, ZN + LONS - 2)
+            for b in range(1, LONS):
+                pl.semaphore_signal(
+                    ready.at[b], inc=1, device_id=peer(z, behind(b)), device_id_type=MESH
+                )
 
         def sends(b, carry):
-            plon = lax.rem(lon + b, LONS)
+            plon = ahead(b)
+
+            @pl.when((q == 0) & (b > 0))
+            def _():
+                pl.semaphore_wait(ready.at[b], 1)
+
             for i in (1, 3, 2, 0):
                 w = lax.rem(z // 2 + i, ZHALF)
                 src = send_a.at[pl.ds((q * LONS + plon) * ZHALF + w, 1)]
@@ -180,6 +193,13 @@
                 else:
                     push_or_keep((b == 0) & (side == parity), src, dst, sa, ra.at[half], 2 * w + side, plon)
             return carry
+
+        @pl.when(q == 0)
+        def _():
+            for i in range(1, QUARTERS):
+                quarter_load(i).start()
+            for copy in weights[3:]:
+                copy.start()
 
         lax.fori_loop(0, LONS, sends, 0)
         return carry
@@ -220,7 +240,8 @@
         lax.fori_loop(0, 2, four, 0)
         dst = out.at[pl.ds((half * WIN + lon) * LONS + parity * ZHALF + z // 2, 1)]
 
-        def forward(j, carry):
+        def forward(step, carry):
+            j = 1 - step
             part = pl.ds(pl.multiple_of(j * ROWS, ROWS), ROWS)
 
             def load():
@@ -239,8 +260,8 @@
             )
 
             def sends(i, carry):
-                b = j * (LONS // 2) + i
-                plon = lax.rem(lon - b + LONS, LONS)
+                b = j * (LONS // 2) + LONS // 2 - 1 - i
+                plon = behind(b)
                 for off in Z_OFFSETS:
                     pz = around(off)
                     src = send_b.at[pl.ds(half * SLABS + b * ZN + pz, 1)]
@@ -289,6 +310,7 @@
             pltpu.SemaphoreType.DMA((HALVES,)),
             pltpu.SemaphoreType.DMA,
             pltpu.SemaphoreType.DMA,
+            pltpu.SemaphoreType.REGULAR((LONS,)),
         ],
         compiler_params=pltpu.CompilerParams(
             collective_id=0, has_side_effects=True, vmem_limit_bytes=48 << 20

time: 62.7 us -> 60.7 us (0.968)
  Pallas kernels: 61.5 us -> 59.6 us
    pallas_call x1, Pallas kernels: 61.5 us -> 59.6 us  [shards(): pl.pallas_call(kernel, out_shape=jax.ShapeDtypeStruct((slabs, WIN, D), BF...]
where the time goes in v4:
time: 60.7 us; the launch traced here: 60.6 us
  Pallas kernels  59.6 us (98%)
  local copies, waits for them, and re-layouts  0.97 us (2%)
    pallas_call x1, Pallas kernels, shards(): pl.pallas_call(kernel, out_shape=jax.ShapeDtypeStruct((slabs, WIN, D), BF...  59.6 us

profile of v4, /device:TPU:32, one launch (start us, length us, event | category | flops | bytes accessed | tf_op | source)
XLA Modules:
  0.0 60.6 jit_solution(17510888678442742774)
XLA Ops:
  0.0 59.6 %shard_map.100 = bf16[128,8,512]{2,1,0:T(8,128)(2,1)S(1)} custom-call(bf16[16,64,512]{2,1,0:T(8,128)(2,1)} %tokens.1, f32[1,512]{1,0:T(1,128)} %bitcast.5, bf16[512,1536]{1,0:T(8,128)(2,1)} %block_qkv.1, bf16[512,512]{1,0:T(8,128)(2,1)} %block_out.1, f32[1,512]{1,0:T(1,128)} %bitcast.6, bf16[512,1536]{1,0:T(8,128)(2,1)} %grid_qkv.1, ...), custom_call_target="tpu_custom_call" | custom-call | tf_op jit(solution)/shard_map/pallas_call | solution.py:295
  59.6 1.0 %copy.12 = bf16[16,64,512]{2,1,0:T(8,128)(2,1)} copy(bf16[16,64,512]{2,1,0:T(8,128)(2,1)S(1)} %bitcast.4) | data formatting | bytes 2097152

commit v5 on v4

--- a/solution.py
+++ b/solution.py
@@ -50,24 +50,32 @@
     k_s[...] = jnp.dot(normed, w_qkv[:, D : 2 * D], preferred_element_type=F32).astype(BF16)
     v_s[...] = jnp.dot(normed, w_qkv[:, 2 * D :], preferred_element_type=F32).astype(BF16)
     masks = head_masks()
-    for w in range(GROUP):
-        rows = slice(w * SPAN, (w + 1) * SPAN)
-        for g in range(HEADS // QUAD):
-            cols = slice(g * LANES, (g + 1) * LANES)
-            q = q_s[rows, cols]
-            diagonal = jnp.concatenate([jnp.where(m, q, jnp.zeros_like(q)) for m in masks], axis=0)
-            scores = lax.dot_general(
-                k_s[rows, cols], diagonal, (((1,), (1,)), ((), ())), preferred_element_type=F32
+    parts = [
+        (slice(w * SPAN, (w + 1) * SPAN), slice(g * LANES, (g + 1) * LANES))
+        for w in range(GROUP)
+        for g in range(HEADS // QUAD)
+    ]
+    scores = []
+    for part in parts:
+        q = q_s[part]
+        diagonal = jnp.concatenate([jnp.where(m, q, jnp.zeros_like(q)) for m in masks], axis=0)
+        scores.append(
+            lax.dot_general(
+                k_s[part], diagonal, (((1,), (1,)), ((), ())), preferred_element_type=F32
             )
-            probs = jnp.exp2(scores - jnp.max(scores, axis=0, keepdims=True))
-            probs = (probs * (1.0 / jnp.sum(probs, axis=0, keepdims=True))).astype(BF16)
-            mixed = lax.dot_general(
-                probs, v_s[rows, cols], (((0,), (0,)), ((), ())), preferred_element_type=F32
-            )
-            kept = mixed[(QUAD - 1) * SPAN :]
-            for h in range(QUAD - 1):
-                kept = jnp.where(masks[h], mixed[h * SPAN : (h + 1) * SPAN], kept)
-            mixed_s[rows, cols] = kept.astype(BF16)
+        )
+    probs = []
+    for score in scores:
+        grown = jnp.exp2(score - jnp.max(score, axis=0, keepdims=True))
+        probs.append((grown * (1.0 / jnp.sum(grown, axis=0, keepdims=True))).astype(BF16))
+    for part, prob in zip(parts, probs):
+        mixed = lax.dot_general(
+            prob, v_s[part], (((0,), (0,)), ((), ())), preferred_element_type=F32
+        )
+        kept = mixed[(QUAD - 1) * SPAN :]
+        for h in range(QUAD - 1):
+            kept = jnp.where(masks[h], mixed[h * SPAN : (h + 1) * SPAN], kept)
+        mixed_s[part] = kept.astype(BF16)
     return load() + jnp.dot(mixed_s[...], w_out[...], preferred_element_type=F32)
 
 
@@ -180,18 +188,19 @@
         def sends(b, carry):
             plon = ahead(b)
 
-            @pl.when((q == 0) & (b > 0))
-            def _():
-                pl.semaphore_wait(ready.at[b], 1)
+            if b:
+                @pl.when(q == 0)
+                def _():
+                    pl.semaphore_wait(ready.at[b], 1)
 
             for i in (1, 3, 2, 0):
                 w = lax.rem(z // 2 + i, ZHALF)
                 src = send_a.at[pl.ds((q * LONS + plon) * ZHALF + w, 1)]
                 dst = recv_a.at[pl.ds(half * SLABS + b * ZN + z, 1)]
-                if i:
+                if i or b:
                     push(src, dst, sa, ra.at[half], 2 * w + side, plon)
                 else:
-                    push_or_keep((b == 0) & (side == parity), src, dst, sa, ra.at[half], 2 * w + side, plon)
+                    push_or_keep(side == parity, src, dst, sa, ra.at[half], 2 * w + side, plon)
             return carry
 
         @pl.when(q == 0)
@@ -201,7 +210,8 @@
             for copy in weights[3:]:
                 copy.start()
 
-        lax.fori_loop(0, LONS, sends, 0)
+        for b in range(LONS):
+            sends(b, 0)
         return carry
 
     lax.fori_loop(0, QUARTERS, block_phase, 0)

time: 60.7 us -> 60.4 us (level)
  no operation moved by 1% of the time
where the time goes in v5:
time: 60.4 us; the launch traced here: 60.3 us
  Pallas kernels  59.4 us (98%)
  local copies, waits for them, and re-layouts  0.97 us (2%)
    pallas_call x1, Pallas kernels, shards(): pl.pallas_call(kernel, out_shape=jax.ShapeDtypeStruct((slabs, WIN, D), BF...  59.4 us

profile of v5, /device:TPU:32, one launch (start us, length us, event | category | flops | bytes accessed | tf_op | source)
XLA Modules:
  0.0 60.3 jit_solution(17067540802537963429)
XLA Ops:
  0.0 59.4 %shard_map.100 = bf16[128,8,512]{2,1,0:T(8,128)(2,1)S(1)} custom-call(bf16[16,64,512]{2,1,0:T(8,128)(2,1)} %tokens.1, f32[1,512]{1,0:T(1,128)} %bitcast.5, bf16[512,1536]{1,0:T(8,128)(2,1)} %block_qkv.1, bf16[512,512]{1,0:T(8,128)(2,1)} %block_out.1, f32[1,512]{1,0:T(1,128)} %bitcast.6, bf16[512,1536]{1,0:T(8,128)(2,1)} %grid_qkv.1, ...), custom_call_target="tpu_custom_call" | custom-call | tf_op jit(solution)/shard_map/pallas_call | solution.py:305
  59.4 1.0 %copy.12 = bf16[16,64,512]{2,1,0:T(8,128)(2,1)} copy(bf16[16,64,512]{2,1,0:T(8,128)(2,1)S(1)} %bitcast.4) | data formatting | bytes 2097152

commit v6 on v5

--- a/solution.py
+++ b/solution.py
@@ -44,7 +44,7 @@
     return [(lane >= h * HEAD) & (lane < (h + 1) * HEAD) for h in range(QUAD)]
 
 
-def attend(load, gain, w_qkv, w_out, q_s, k_s, v_s, mixed_s):
+def attend(load, gain, w_qkv, w_out, q_s, k_s, v_s, mixed_s, before_out=lambda: None):
     normed = norm(load(), gain[...])
     q_s[...] = (jnp.dot(normed, w_qkv[:, :D], preferred_element_type=F32) * SCALE).astype(BF16)
     k_s[...] = jnp.dot(normed, w_qkv[:, D : 2 * D], preferred_element_type=F32).astype(BF16)
@@ -76,6 +76,7 @@
         for h in range(QUAD - 1):
             kept = jnp.where(masks[h], mixed[h * SPAN : (h + 1) * SPAN], kept)
         mixed_s[part] = kept.astype(BF16)
+    before_out()
     return load() + jnp.dot(mixed_s[...], w_out[...], preferred_element_type=F32)
 
 
@@ -171,19 +172,20 @@
                 [tile[:, w * WIN : (w + 1) * WIN, :].reshape(SPAN, D) for w in range(GROUP)], axis=0
             )
 
-        result = attend(load, g1, wq1, wo1, q_s, k_s, v_s, mixed_s)
+        def entry():
+            @pl.when(q == 0)
+            def _():
+                pl.semaphore_wait(barrier, ZN + LONS - 2)
+                for b in range(1, LONS):
+                    pl.semaphore_signal(
+                        ready.at[b], inc=1, device_id=peer(z, behind(b)), device_id_type=MESH
+                    )
+
+        result = attend(load, g1, wq1, wo1, q_s, k_s, v_s, mixed_s, entry)
         for w in range(GROUP):
             part = result[w * SPAN : (w + 1) * SPAN].reshape(WIN, WIN, D)
             for r in range(WIN):
                 send_a[(q * LONS + r) * ZHALF + w] = part[r].astype(BF16)
-
-        @pl.when(q == 0)
-        def _():
-            pl.semaphore_wait(barrier, ZN + LONS - 2)
-            for b in range(1, LONS):
-                pl.semaphore_signal(
-                    ready.at[b], inc=1, device_id=peer(z, behind(b)), device_id_type=MESH
-                )
 
         def sends(b, carry):
             plon = ahead(b)
@@ -269,19 +271,15 @@
                 total.astype(BF16).reshape(ROWS // WIN, WIN, D)
             )
 
-            def sends(i, carry):
-                b = j * (LONS // 2) + LONS // 2 - 1 - i
-                plon = behind(b)
-                for off in Z_OFFSETS:
-                    pz = around(off)
+            for off in Z_OFFSETS:
+                pz = around(off)
+                for i in range(LONS // 2):
+                    b = j * (LONS // 2) + LONS // 2 - 1 - i
                     src = send_b.at[pl.ds(half * SLABS + b * ZN + pz, 1)]
                     if off:
-                        push(src, dst, sb, rb, pz, plon)
+                        push(src, dst, sb, rb, pz, behind(b))
                     else:
-                        push_or_keep(b == 0, src, dst, sb, rb, pz, plon)
-                return carry
-
-            lax.fori_loop(0, LONS // 2, sends, 0)
+                        push_or_keep(b == 0, src, dst, sb, rb, pz, behind(b))
             return carry
 
         lax.fori_loop(0, 2, forward, 0)

time: 60.4 us -> 60.2 us (level)
  no operation moved by 1% of the time
where the time goes in v6:
time: 60.2 us; the launch traced here: 60.1 us
  Pallas kernels  59.1 us (98%)
  local copies, waits for them, and re-layouts  0.97 us (2%)
    pallas_call x1, Pallas kernels, shards(): pl.pallas_call(kernel, out_shape=jax.ShapeDtypeStruct((slabs, WIN, D), BF...  59.1 us

profile of v6, /device:TPU:32, one launch (start us, length us, event | category | flops | bytes accessed | tf_op | source)
XLA Modules:
  0.0 60.1 jit_solution(15696788737599692501)
XLA Ops:
  0.0 59.1 %shard_map.100 = bf16[128,8,512]{2,1,0:T(8,128)(2,1)S(1)} custom-call(bf16[16,64,512]{2,1,0:T(8,128)(2,1)} %tokens.1, f32[1,512]{1,0:T(1,128)} %bitcast.5, bf16[512,1536]{1,0:T(8,128)(2,1)} %block_qkv.1, bf16[512,512]{1,0:T(8,128)(2,1)} %block_out.1, f32[1,512]{1,0:T(1,128)} %bitcast.6, bf16[512,1536]{1,0:T(8,128)(2,1)} %grid_qkv.1, ...), custom_call_target="tpu_custom_call" | custom-call | tf_op jit(solution)/shard_map/pallas_call | solution.py:303
  59.1 1.0 %copy.12 = bf16[16,64,512]{2,1,0:T(8,128)(2,1)} copy(bf16[16,64,512]{2,1,0:T(8,128)(2,1)S(1)} %bitcast.4) | data formatting | bytes 2097152

commit v7 on v6

--- a/solution.py
+++ b/solution.py
@@ -271,15 +271,19 @@
                 total.astype(BF16).reshape(ROWS // WIN, WIN, D)
             )
 
-            for off in Z_OFFSETS:
-                pz = around(off)
-                for i in range(LONS // 2):
-                    b = j * (LONS // 2) + LONS // 2 - 1 - i
+            def sends(i, carry):
+                b = j * (LONS // 2) + LONS // 2 - 1 - i
+                plon = behind(b)
+                for off in Z_OFFSETS:
+                    pz = around(off)
                     src = send_b.at[pl.ds(half * SLABS + b * ZN + pz, 1)]
                     if off:
-                        push(src, dst, sb, rb, pz, behind(b))
+                        push(src, dst, sb, rb, pz, plon)
                     else:
-                        push_or_keep(b == 0, src, dst, sb, rb, pz, behind(b))
+                        push_or_keep(b == 0, src, dst, sb, rb, pz, plon)
+                return carry
+
+            lax.fori_loop(0, LONS // 2, sends, 0)
             return carry
 
         lax.fori_loop(0, 2, forward, 0)

time: 60.2 us -> 60.6 us (level)
  no operation moved by 1% of the time
where the time goes in v7:
time: 60.6 us; the launch traced here: 60.5 us
  Pallas kernels  59.5 us (98%)
  local copies, waits for them, and re-layouts  0.97 us (2%)
    pallas_call x1, Pallas kernels, shards(): pl.pallas_call(kernel, out_shape=jax.ShapeDtypeStruct((slabs, WIN, D), BF...  59.5 us

profile of v7, /device:TPU:32, one launch (start us, length us, event | category | flops | bytes accessed | tf_op | source)
XLA Modules:
  0.0 60.5 jit_solution(17701668180300750451)
XLA Ops:
  0.0 59.5 %shard_map.100 = bf16[128,8,512]{2,1,0:T(8,128)(2,1)S(1)} custom-call(bf16[16,64,512]{2,1,0:T(8,128)(2,1)} %tokens.1, f32[1,512]{1,0:T(1,128)} %bitcast.5, bf16[512,1536]{1,0:T(8,128)(2,1)} %block_qkv.1, bf16[512,512]{1,0:T(8,128)(2,1)} %block_out.1, f32[1,512]{1,0:T(1,128)} %bitcast.6, bf16[512,1536]{1,0:T(8,128)(2,1)} %grid_qkv.1, ...), custom_call_target="tpu_custom_call" | custom-call | tf_op jit(solution)/shard_map/pallas_call | solution.py:307
  59.5 1.0 %copy.12 = bf16[16,64,512]{2,1,0:T(8,128)(2,1)} copy(bf16[16,64,512]{2,1,0:T(8,128)(2,1)S(1)} %bitcast.4) | data formatting | bytes 2097152
